TPU v7x, 32 devices: a whole 2x2x4 slice. The times are simulated.
32 devices in a mesh: seq: 16 (over z, y, x), head: 2 (over core).
Axes of the slice: x: 2, y: 2, z: 4, core: 2. Of those that a mesh axis runs over, the one named last changes fastest.
Arguments:
- queries: bfloat16 [512, 4096], P('seq', 'head'), may hold values from -6 to 6
- cache_keys: bfloat16 [65536, 1024], P('seq', 'head'), may hold values from -8 to 8
- cache_values: bfloat16 [65536, 1024], P('seq', 'head'), may hold values from -8 to 8
- new_keys: bfloat16 [512, 1024], P('seq', 'head'), may hold values from -8 to 8
- new_values: bfloat16 [512, 1024], P('seq', 'head'), may hold values from -8 to 8
- new_pos: int32 [512], replicated, may hold values from 0 to 511, as said below
- residual: bfloat16 [512, 4096], P('head', 'seq'), may hold values from -6 to 6
- out_weight: bfloat16 [4096, 4096], P('head', 'seq'), may hold values from -0.09375 to 0.09375
Outputs:
- attended: bfloat16 [512, 4096], P('seq', 'head')
- hidden: bfloat16 [512, 4096], P('head', 'seq')
Inputs may be any that keep to these rules, and one draw needn't show every extreme that they name: `new_pos`: each number of 0 to 511 appears exactly once.
All inputs are finite; a program needn't handle non-finite values.
Results may differ from a plain program's by a relative error of at most 0.0095.
Values may be sent and summed in bfloat16 or wider, within the bound.
A program may use at most 128 MiB of HBM per device.

v0:
```python
import math

import jax
import jax.numpy as jnp
from jax import lax
from jax.sharding import PartitionSpec as P

HD = 128
TURN = 128


rope_base = 3580165449.0


def rotate(vectors, offsets):
    half_width = vectors.shape[-1] // 2
    frequency = jnp.exp(
        jnp.arange(half_width, dtype=jnp.float32) * (-2.0 * math.log(rope_base) / vectors.shape[-1])
    )
    angles = offsets.astype(jnp.float32)[:, None] * frequency[None, :]
    cosine = jnp.concatenate([jnp.cos(angles), jnp.cos(angles)], axis=-1)[:, None, :]
    sine_part = jnp.concatenate([jnp.sin(angles), jnp.sin(angles)], axis=-1)[:, None, :]
    turned = jnp.concatenate([-vectors[..., half_width:], vectors[..., :half_width]], axis=-1)
    return vectors * cosine + turned * sine_part


def fold_scores(carry, scores, value_block, visible):
    running_max, running_sum, running_out = carry
    new_max = jnp.maximum(running_max, jnp.max(scores, axis=-1))
    shrink = jnp.exp(running_max - new_max)
    exps = jnp.exp(scores - new_max[..., None])
    if visible is not None:
        exps = jnp.where(visible, exps, 0.0)
    running_sum = running_sum * shrink + jnp.sum(exps, axis=-1)
    product = jnp.einsum(
        "grk,kgd->grd", exps.astype(jnp.bfloat16), value_block, preferred_element_type=jnp.float32
    )
    running_out = running_out * shrink[..., None] + product
    return (new_max, running_sum, running_out)


def on_device(
    queries, cache_keys, cache_values, new_keys, new_values, new_pos, residual, out_weight
):
    local_rows = queries.shape[0]
    kv_local = cache_keys.shape[1] // HD
    group_size = queries.shape[1] // cache_keys.shape[1]
    offsets = new_pos % TURN
    turn_ids = new_pos // TURN
    row_start = lax.axis_index("seq") * local_rows
    own_offsets = lax.dynamic_slice_in_dim(offsets, row_start, local_rows)
    own_turns = lax.dynamic_slice_in_dim(turn_ids, row_start, local_rows)
    query_rot = rotate(
        queries.astype(jnp.float32).reshape(local_rows, kv_local * group_size, HD), own_offsets
    )
    query_rot = query_rot.astype(jnp.bfloat16).reshape(local_rows, kv_local * group_size * HD)
    key_rot = rotate(
        new_keys.astype(jnp.float32).reshape(local_rows, kv_local, HD), own_offsets
    ).astype(jnp.bfloat16)
    all_queries = lax.all_gather(query_rot, "seq", axis=0, tiled=True)
    total_rows = all_queries.shape[0]
    head_local = kv_local * group_size
    grouped = (
        all_queries.reshape(total_rows, kv_local, group_size, HD)
        .transpose(1, 0, 2, 3)
        .reshape(kv_local, total_rows * group_size, HD)
    )
    score_scale = 1.0 / math.sqrt(HD)
    block_rows = min(512, cache_keys.shape[0])
    block_count = cache_keys.shape[0] // block_rows
    key_blocks = cache_keys.reshape(block_count, block_rows, kv_local, HD)
    value_blocks = cache_values.reshape(block_count, block_rows, kv_local, HD)

    def absorb(carry, blocks):
        scores = (
            jnp.einsum("grd,kgd->grk", grouped, blocks[0], preferred_element_type=jnp.float32)
            * score_scale
        )
        return (fold_scores(carry, scores, blocks[1], None), None)

    start_max = jnp.full((kv_local, total_rows * group_size), -1e30, jnp.float32)
    start_sum = jnp.zeros((kv_local, total_rows * group_size), jnp.float32)
    start_out = jnp.zeros((kv_local, total_rows * group_size, HD), jnp.float32)
    carry, unused = lax.scan(absorb, (start_max, start_sum, start_out), (key_blocks, value_blocks))
    visible = (turn_ids[:, None] == own_turns[None, :]) & (own_offsets[None, :] <= offsets[:, None])
    visible = jnp.repeat(visible, group_size, axis=0)[None]
    scores = (
        jnp.einsum("grd,kgd->grk", grouped, key_rot, preferred_element_type=jnp.float32)
        * score_scale
    )
    masked = jnp.where(visible, scores, -1e30)
    value_new = new_values.reshape(local_rows, kv_local, HD)
    running_max, running_sum, running_out = fold_scores(carry, masked, value_new, visible)
    out_rows = (
        running_out.reshape(kv_local, total_rows, group_size, HD)
        .transpose(1, 0, 2, 3)
        .reshape(total_rows, head_local * HD)
    )
    max_rows = (
        running_max.reshape(kv_local, total_rows, group_size)
        .transpose(1, 0, 2)
        .reshape(total_rows, head_local)
    )
    sum_rows = (
        running_sum.reshape(kv_local, total_rows, group_size)
        .transpose(1, 0, 2)
        .reshape(total_rows, head_local)
    )
    partials, maxima, totals = (
        lax.all_to_all(out_rows[None], "seq", split_axis=1, concat_axis=0, tiled=True),
        lax.all_to_all(max_rows[None], "seq", split_axis=1, concat_axis=0, tiled=True),
        lax.all_to_all(sum_rows[None], "seq", split_axis=1, concat_axis=0, tiled=True),
    )
    peak_score = jnp.max(maxima, axis=0)
    weight = jnp.exp(maxima - peak_score[None])
    numerator = jnp.sum(
        partials.reshape(partials.shape[0], local_rows, head_local, HD) * weight[..., None], axis=0
    )
    denominator = jnp.sum(totals * weight, axis=0)
    attended = (
        (numerator / denominator[..., None])
        .reshape(local_rows, head_local * HD)
        .astype(jnp.bfloat16)
    )
    projected = jnp.dot(
        lax.all_gather(attended, "seq", axis=0, tiled=True),
        out_weight,
        preferred_element_type=jnp.float32,
    )
    summed = lax.psum_scatter(
        projected.astype(jnp.bfloat16), "head", scatter_dimension=0, tiled=True
    ).astype(jnp.float32)
    hidden = (residual.astype(jnp.float32) + summed).astype(jnp.bfloat16)
    return (attended, hidden)


def solution(mesh):
    return jax.shard_map(
        on_device,
        mesh=mesh,
        in_specs=(
            P("seq", "head"),
            P("seq", "head"),
            P("seq", "head"),
            P("seq", "head"),
            P("seq", "head"),
            P(),
            P("head", "seq"),
            P("head", "seq"),
        ),
        out_specs=(P("seq", "head"), P("head", "seq")),
        check_vma=False,
    )
```

profile of v0, /device:TPU:0, one launch (start us, length us, event | category | flops | bytes accessed | tf_op | source)
XLA Modules:
  0.0 543.2 jit_solution(13183920415960751291)
XLA Ops:
  7.2 1.0 convert_bitcast_fusion
  9.6 1.7 fusion.21
  11.4 6.9 %reshape.119 = bf16[8,512,4,128]{3,2,1,0:T(4,128)(2,1)} reshape(bf16[4096,512]{1,0:T(8,128)(2,1)} %param.11) | data formatting | bytes 8388608 | tf_op jit(solution)/shard_map/reshape | solution.py:71
  18.3 7.0 %reshape.120 = bf16[8,512,4,128]{3,2,1,0:T(4,128)(2,1)} reshape(bf16[4096,512]{1,0:T(8,128)(2,1)} %param.12) | data formatting | bytes 8388608 | tf_op jit(solution)/shard_map/reshape | solution.py:72
  26.3 48.6 %all-gather.3.cloned.1.call-done = bf16[512,2048]{1,0:T(8,128)(2,1)} async-done(((bf16[32,2048]{1,0:T(8,128)(2,1)}), bf16[512,2048]{1,0:T(8,128)(2,1)}) %all-gather.3.cloned.1.call-update) | async-done | bytes 2097168 | tf_op jit(solution)/shard_map/all_gather | solution.py:60
  74.9 4.4 reshape.108
  79.4 2.3 copy.91
  81.7 237.0 %while.15 = (s32[]{:T(128)}, f32[4,2048]{1,0:T(4,128)S(1)}, f32[4,2048]{1,0:T(4,128)S(1)}, f32[4,2048,128]{2,1,0:T(8,128)}, bf16[8,512,4,128]{3,2,1,0:T(4,128)(2...) while((s32[]{:T(128)}, f32[4,2048]{1,0:T(4,128)S(1)}, ...), condition=%wide.region_3.4_spmd.clone, body=%wide.region_0.3_spmd.clone.sunk | while | flops 2184224768 | bytes 66584716 | solution.py:84
  81.7 2.4 constant_dynamic-slice_fusion.3
  84.1 8.1 %bitcast_reduce_fusion.2 = (f32[4,2048]{1,0:T(4,128)S(1)}, f32[4,512,2048]{2,1,0:T(8,128)}) fusion(bf16[4,2048,128]{2,1,0:T(8,128)(2,1)S(1)} %get-tuple-element.219, bf16[1,512,4,128]{3,2,1,0:T(4,128)(2,1)S(1)} %get-tuple-element.190), kind=kOutput, calls=%fused_computation.1.clone.1 | convolution fusion | flops 1082122240 | bytes 19431424 | tf_op jit(solution)/shard_map/while/body/eval_jaxpr/grd,kgd->grk/dot_general | solution.py:76
  92.2 8.6 %fusion.47 = f32[4,2048]{1,0:T(4,128)S(1)} fusion(f32[4,512,2048]{2,1,0:T(8,128)} %get-tuple-element.192, f32[4,2048]{1,0:T(4,128)S(1)} %select_maximum_fusion.2), kind=kLoop, calls=%fused_computation.4.clone.1 | loop fusion | flops 12574720 | bytes 16842752 | tf_op jit(solution)/shard_map/while/body/eval_jaxpr/reduce_sum | solution.py:34
  100.9 9.4 %fusion.49 = f32[4,2048,128]{2,1,0:T(8,128)} fusion(f32[4,2048,128]{2,1,0:T(8,128)} %get-tuple-element.208, f32[4,512,2048]{2,1,0:T(8,128)} %get-tuple-element.192, f32[4,2048]{1,0:T(4,128)S(1)} %select_maximum_fusion.2, f32[4,2048]{1,0:T(4,128)S(1)} %get-tuple-element.194, pred[]{:T(512)S(6)} %compare.6, bf16[1,512,4,128]{3,2,1,0:T(4,128)(2,1)S(1)} %copy-done.1), kind=kOutput, calls=%fused_computation.9.clone.1 | convolution fusion | flops 1089470464 | bytes 25755648 | tf_op jit(solution)/shard_map/while/body/eval_jaxpr/grk,kgd->grd/dot_general | solution.py:35
  110.3 2.4 constant_dynamic-slice_fusion.3
  112.7 8.1 %bitcast_reduce_fusion.2 = (f32[4,2048]{1,0:T(4,128)S(1)}, f32[4,512,2048]{2,1,0:T(8,128)}) fusion(bf16[4,2048,128]{2,1,0:T(8,128)(2,1)S(1)} %get-tuple-element.219, bf16[1,512,4,128]{3,2,1,0:T(4,128)(2,1)S(1)} %get-tuple-element.190), kind=kOutput, calls=%fused_computation.1.clone.1 | convolution fusion | flops 1082122240 | bytes 19431424 | tf_op jit(solution)/shard_map/while/body/eval_jaxpr/grd,kgd->grk/dot_general | solution.py:76
  120.8 8.6 %fusion.47 = f32[4,2048]{1,0:T(4,128)S(1)} fusion(f32[4,512,2048]{2,1,0:T(8,128)} %get-tuple-element.192, f32[4,2048]{1,0:T(4,128)S(1)} %select_maximum_fusion.2), kind=kLoop, calls=%fused_computation.4.clone.1 | loop fusion | flops 12574720 | bytes 16842752 | tf_op jit(solution)/shard_map/while/body/eval_jaxpr/reduce_sum | solution.py:34
  129.5 10.6 %fusion.49 = f32[4,2048,128]{2,1,0:T(8,128)} fusion(f32[4,2048,128]{2,1,0:T(8,128)} %get-tuple-element.208, f32[4,512,2048]{2,1,0:T(8,128)} %get-tuple-element.192, f32[4,2048]{1,0:T(4,128)S(1)} %select_maximum_fusion.2, f32[4,2048]{1,0:T(4,128)S(1)} %get-tuple-element.194, pred[]{:T(512)S(6)} %compare.6, bf16[1,512,4,128]{3,2,1,0:T(4,128)(2,1)S(1)} %copy-done.1), kind=kOutput, calls=%fused_computation.9.clone.1 | convolution fusion | flops 1089470464 | bytes 25755648 | tf_op jit(solution)/shard_map/while/body/eval_jaxpr/grk,kgd->grd/dot_general | solution.py:35
  140.1 2.4 constant_dynamic-slice_fusion.3
  142.5 8.1 %bitcast_reduce_fusion.2 = (f32[4,2048]{1,0:T(4,128)S(1)}, f32[4,512,2048]{2,1,0:T(8,128)}) fusion(bf16[4,2048,128]{2,1,0:T(8,128)(2,1)S(1)} %get-tuple-element.219, bf16[1,512,4,128]{3,2,1,0:T(4,128)(2,1)S(1)} %get-tuple-element.190), kind=kOutput, calls=%fused_computation.1.clone.1 | convolution fusion | flops 1082122240 | bytes 19431424 | tf_op jit(solution)/shard_map/while/body/eval_jaxpr/grd,kgd->grk/dot_general | solution.py:76
  150.6 8.6 %fusion.47 = f32[4,2048]{1,0:T(4,128)S(1)} fusion(f32[4,512,2048]{2,1,0:T(8,128)} %get-tuple-element.192, f32[4,2048]{1,0:T(4,128)S(1)} %select_maximum_fusion.2), kind=kLoop, calls=%fused_computation.4.clone.1 | loop fusion | flops 12574720 | bytes 16842752 | tf_op jit(solution)/shard_map/while/body/eval_jaxpr/reduce_sum | solution.py:34
  159.3 10.6 %fusion.49 = f32[4,2048,128]{2,1,0:T(8,128)} fusion(f32[4,2048,128]{2,1,0:T(8,128)} %get-tuple-element.208, f32[4,512,2048]{2,1,0:T(8,128)} %get-tuple-element.192, f32[4,2048]{1,0:T(4,128)S(1)} %select_maximum_fusion.2, f32[4,2048]{1,0:T(4,128)S(1)} %get-tuple-element.194, pred[]{:T(512)S(6)} %compare.6, bf16[1,512,4,128]{3,2,1,0:T(4,128)(2,1)S(1)} %copy-done.1), kind=kOutput, calls=%fused_computation.9.clone.1 | convolution fusion | flops 1089470464 | bytes 25755648 | tf_op jit(solution)/shard_map/while/body/eval_jaxpr/grk,kgd->grd/dot_general | solution.py:35
  169.8 2.4 constant_dynamic-slice_fusion.3
  172.2 8.1 %bitcast_reduce_fusion.2 = (f32[4,2048]{1,0:T(4,128)S(1)}, f32[4,512,2048]{2,1,0:T(8,128)}) fusion(bf16[4,2048,128]{2,1,0:T(8,128)(2,1)S(1)} %get-tuple-element.219, bf16[1,512,4,128]{3,2,1,0:T(4,128)(2,1)S(1)} %get-tuple-element.190), kind=kOutput, calls=%fused_computation.1.clone.1 | convolution fusion | flops 1082122240 | bytes 19431424 | tf_op jit(solution)/shard_map/while/body/eval_jaxpr/grd,kgd->grk/dot_general | solution.py:76
  180.3 8.6 %fusion.47 = f32[4,2048]{1,0:T(4,128)S(1)} fusion(f32[4,512,2048]{2,1,0:T(8,128)} %get-tuple-element.192, f32[4,2048]{1,0:T(4,128)S(1)} %select_maximum_fusion.2), kind=kLoop, calls=%fused_computation.4.clone.1 | loop fusion | flops 12574720 | bytes 16842752 | tf_op jit(solution)/shard_map/while/body/eval_jaxpr/reduce_sum | solution.py:34
  189.0 10.6 %fusion.49 = f32[4,2048,128]{2,1,0:T(8,128)} fusion(f32[4,2048,128]{2,1,0:T(8,128)} %get-tuple-element.208, f32[4,512,2048]{2,1,0:T(8,128)} %get-tuple-element.192, f32[4,2048]{1,0:T(4,128)S(1)} %select_maximum_fusion.2, f32[4,2048]{1,0:T(4,128)S(1)} %get-tuple-element.194, pred[]{:T(512)S(6)} %compare.6, bf16[1,512,4,128]{3,2,1,0:T(4,128)(2,1)S(1)} %copy-done.1), kind=kOutput, calls=%fused_computation.9.clone.1 | convolution fusion | flops 1089470464 | bytes 25755648 | tf_op jit(solution)/shard_map/while/body/eval_jaxpr/grk,kgd->grd/dot_general | solution.py:35
  199.6 2.4 constant_dynamic-slice_fusion.3
  202.0 8.1 %bitcast_reduce_fusion.2 = (f32[4,2048]{1,0:T(4,128)S(1)}, f32[4,512,2048]{2,1,0:T(8,128)}) fusion(bf16[4,2048,128]{2,1,0:T(8,128)(2,1)S(1)} %get-tuple-element.219, bf16[1,512,4,128]{3,2,1,0:T(4,128)(2,1)S(1)} %get-tuple-element.190), kind=kOutput, calls=%fused_computation.1.clone.1 | convolution fusion | flops 1082122240 | bytes 19431424 | tf_op jit(solution)/shard_map/while/body/eval_jaxpr/grd,kgd->grk/dot_general | solution.py:76
  210.1 8.6 %fusion.47 = f32[4,2048]{1,0:T(4,128)S(1)} fusion(f32[4,512,2048]{2,1,0:T(8,128)} %get-tuple-element.192, f32[4,2048]{1,0:T(4,128)S(1)} %select_maximum_fusion.2), kind=kLoop, calls=%fused_computation.4.clone.1 | loop fusion | flops 12574720 | bytes 16842752 | tf_op jit(solution)/shard_map/while/body/eval_jaxpr/reduce_sum | solution.py:34
  218.8 10.6 %fusion.49 = f32[4,2048,128]{2,1,0:T(8,128)} fusion(f32[4,2048,128]{2,1,0:T(8,128)} %get-tuple-element.208, f32[4,512,2048]{2,1,0:T(8,128)} %get-tuple-element.192, f32[4,2048]{1,0:T(4,128)S(1)} %select_maximum_fusion.2, f32[4,2048]{1,0:T(4,128)S(1)} %get-tuple-element.194, pred[]{:T(512)S(6)} %compare.6, bf16[1,512,4,128]{3,2,1,0:T(4,128)(2,1)S(1)} %copy-done.1), kind=kOutput, calls=%fused_computation.9.clone.1 | convolution fusion | flops 1089470464 | bytes 25755648 | tf_op jit(solution)/shard_map/while/body/eval_jaxpr/grk,kgd->grd/dot_general | solution.py:35
  229.4 2.4 constant_dynamic-slice_fusion.3
  231.8 8.1 %bitcast_reduce_fusion.2 = (f32[4,2048]{1,0:T(4,128)S(1)}, f32[4,512,2048]{2,1,0:T(8,128)}) fusion(bf16[4,2048,128]{2,1,0:T(8,128)(2,1)S(1)} %get-tuple-element.219, bf16[1,512,4,128]{3,2,1,0:T(4,128)(2,1)S(1)} %get-tuple-element.190), kind=kOutput, calls=%fused_computation.1.clone.1 | convolution fusion | flops 1082122240 | bytes 19431424 | tf_op jit(solution)/shard_map/while/body/eval_jaxpr/grd,kgd->grk/dot_general | solution.py:76
  239.9 8.6 %fusion.47 = f32[4,2048]{1,0:T(4,128)S(1)} fusion(f32[4,512,2048]{2,1,0:T(8,128)} %get-tuple-element.192, f32[4,2048]{1,0:T(4,128)S(1)} %select_maximum_fusion.2), kind=kLoop, calls=%fused_computation.4.clone.1 | loop fusion | flops 12574720 | bytes 16842752 | tf_op jit(solution)/shard_map/while/body/eval_jaxpr/reduce_sum | solution.py:34
  248.6 10.6 %fusion.49 = f32[4,2048,128]{2,1,0:T(8,128)} fusion(f32[4,2048,128]{2,1,0:T(8,128)} %get-tuple-element.208, f32[4,512,2048]{2,1,0:T(8,128)} %get-tuple-element.192, f32[4,2048]{1,0:T(4,128)S(1)} %select_maximum_fusion.2, f32[4,2048]{1,0:T(4,128)S(1)} %get-tuple-element.194, pred[]{:T(512)S(6)} %compare.6, bf16[1,512,4,128]{3,2,1,0:T(4,128)(2,1)S(1)} %copy-done.1), kind=kOutput, calls=%fused_computation.9.clone.1 | convolution fusion | flops 1089470464 | bytes 25755648 | tf_op jit(solution)/shard_map/while/body/eval_jaxpr/grk,kgd->grd/dot_general | solution.py:35
  259.1 2.4 constant_dynamic-slice_fusion.3
  261.5 8.1 %bitcast_reduce_fusion.2 = (f32[4,2048]{1,0:T(4,128)S(1)}, f32[4,512,2048]{2,1,0:T(8,128)}) fusion(bf16[4,2048,128]{2,1,0:T(8,128)(2,1)S(1)} %get-tuple-element.219, bf16[1,512,4,128]{3,2,1,0:T(4,128)(2,1)S(1)} %get-tuple-element.190), kind=kOutput, calls=%fused_computation.1.clone.1 | convolution fusion | flops 1082122240 | bytes 19431424 | tf_op jit(solution)/shard_map/while/body/eval_jaxpr/grd,kgd->grk/dot_general | solution.py:76
  269.6 8.6 %fusion.47 = f32[4,2048]{1,0:T(4,128)S(1)} fusion(f32[4,512,2048]{2,1,0:T(8,128)} %get-tuple-element.192, f32[4,2048]{1,0:T(4,128)S(1)} %select_maximum_fusion.2), kind=kLoop, calls=%fused_computation.4.clone.1 | loop fusion | flops 12574720 | bytes 16842752 | tf_op jit(solution)/shard_map/while/body/eval_jaxpr/reduce_sum | solution.py:34
  278.3 10.6 %fusion.49 = f32[4,2048,128]{2,1,0:T(8,128)} fusion(f32[4,2048,128]{2,1,0:T(8,128)} %get-tuple-element.208, f32[4,512,2048]{2,1,0:T(8,128)} %get-tuple-element.192, f32[4,2048]{1,0:T(4,128)S(1)} %select_maximum_fusion.2, f32[4,2048]{1,0:T(4,128)S(1)} %get-tuple-element.194, pred[]{:T(512)S(6)} %compare.6, bf16[1,512,4,128]{3,2,1,0:T(4,128)(2,1)S(1)} %copy-done.1), kind=kOutput, calls=%fused_computation.9.clone.1 | convolution fusion | flops 1089470464 | bytes 25755648 | tf_op jit(solution)/shard_map/while/body/eval_jaxpr/grk,kgd->grd/dot_general | solution.py:35
  288.9 2.4 constant_dynamic-slice_fusion.3
  291.3 8.1 %bitcast_reduce_fusion.2 = (f32[4,2048]{1,0:T(4,128)S(1)}, f32[4,512,2048]{2,1,0:T(8,128)}) fusion(bf16[4,2048,128]{2,1,0:T(8,128)(2,1)S(1)} %get-tuple-element.219, bf16[1,512,4,128]{3,2,1,0:T(4,128)(2,1)S(1)} %get-tuple-element.190), kind=kOutput, calls=%fused_computation.1.clone.1 | convolution fusion | flops 1082122240 | bytes 19431424 | tf_op jit(solution)/shard_map/while/body/eval_jaxpr/grd,kgd->grk/dot_general | solution.py:76
  299.4 8.6 %fusion.47 = f32[4,2048]{1,0:T(4,128)S(1)} fusion(f32[4,512,2048]{2,1,0:T(8,128)} %get-tuple-element.192, f32[4,2048]{1,0:T(4,128)S(1)} %select_maximum_fusion.2), kind=kLoop, calls=%fused_computation.4.clone.1 | loop fusion | flops 12574720 | bytes 16842752 | tf_op jit(solution)/shard_map/while/body/eval_jaxpr/reduce_sum | solution.py:34
  308.1 10.6 %fusion.49 = f32[4,2048,128]{2,1,0:T(8,128)} fusion(f32[4,2048,128]{2,1,0:T(8,128)} %get-tuple-element.208, f32[4,512,2048]{2,1,0:T(8,128)} %get-tuple-element.192, f32[4,2048]{1,0:T(4,128)S(1)} %select_maximum_fusion.2, f32[4,2048]{1,0:T(4,128)S(1)} %get-tuple-element.194, pred[]{:T(512)S(6)} %compare.6, bf16[1,512,4,128]{3,2,1,0:T(4,128)(2,1)S(1)} %copy-done.1), kind=kOutput, calls=%fused_computation.9.clone.1 | convolution fusion | flops 1089470464 | bytes 25755648 | tf_op jit(solution)/shard_map/while/body/eval_jaxpr/grk,kgd->grd/dot_general | solution.py:35
  318.7 0.9 fusion.34
  319.6 0.9 copy-done.3
  320.9 1.1 reshape.116
  323.0 1.3 reduce.1
  324.2 0.8 reshape.124
  325.0 4.3 all-to-all-start.2
  329.3 1.1 reshape.115
  330.9 1.3 reduce.3
  332.1 0.8 reshape.122
  332.9 3.8 all-to-all-done.2
  336.7 3.5 all-to-all-start.1
  340.2 4.8 multiply_add_fusion
  345.0 5.2 copy.101
  350.2 11.0 %copy.102 = f32[1,512,2048]{2,0,1:T(1,128)} copy(f32[1,512,2048]{1,2,0:T(8,128)} %bitcast.95) | data formatting | bytes 8388608 | tf_op jit(solution)/shard_map/broadcast_in_dim;reshape | solution.py:110
  361.2 6.9 %all-to-all-start = ((f32[1,512,2048]{2,0,1:T(1,128)}), f32[1,512,2048]{2,0,1:T(1,128)}, u32[]{:S(2)}, u32[]{:S(2)}) async-start(f32[1,512,2048]{2,0,1:T(1,128)} %copy.102), calls=%async_computation | async-start | bytes 8388608 | tf_op jit(solution)/shard_map/all_to_all | solution.py:110
  371.2 2.6 mul.149
  373.8 4.9 mul.150
  378.8 67.2 %all-to-all-done = f32[1,512,2048]{2,0,1:T(1,128)} async-done(((f32[1,512,2048]{2,0,1:T(1,128)}), f32[1,512,2048]{2,0,1:T(1,128)}, u32[]{:S(2)}, u32[]{:S(2)}) %all-to-all-start) | async-done | bytes 4194336 | tf_op jit(solution)/shard_map/all_to_all | solution.py:110
  446.0 4.3 copy.119
  450.3 0.9 multiply_reduce_fusion
  452.2 73.4 %all-gather.5.cloned.1.call-done = bf16[512,2048]{1,0:T(8,128)(2,1)} async-done(((bf16[32,2048]{1,0:T(8,128)(2,1)}), bf16[512,2048]{1,0:T(8,128)(2,1)}) %all-gather.5.cloned.1.call-update) | async-done | bytes 2097168 | tf_op jit(solution)/shard_map/all_gather | solution.py:126
  525.6 3.0 convolution_convert_fusion
  528.7 6.5 %reduce-scatter.2.cloned.1.call-done = bf16[256,256]{1,0:T(8,128)(2,1)} async-done(((bf16[512,256]{1,0:T(8,128)(2,1)}), bf16[256,256]{1,0:T(8,128)(2,1)}) %reduce-scatter.2.cloned.1.call-update) | async-done | bytes 131088 | tf_op jit(solution)/shard_map/reduce_scatter | solution.py:130
  535.1 1.6 add_convert_fusion
  (102 shorter events, 8.8 us)
Async XLA Ops:
  7.2 518.4 %copy-start = (bf16[2048,256]{1,0:T(8,128)(2,1)S(1)}, bf16[2048,256]{1,0:T(8,128)(2,1)}, u32[]{:S(2)}) copy-start(bf16[2048,256]{1,0:T(8,128)(2,1)} %param.17) | copy-start | bytes 3145732
  7.2 67.8 %all-gather.3.cloned.1.call-start = ((), (), s32[]{:S(2)}) async-start(), calls=%async_computation.4 | async-start | bytes 2228224 | tf_op jit(solution)/shard_map/all_gather | solution.py:60
  18.3 7.9 %copy-start.5 = (bf16[32,512]{1,0:T(8,128)(2,1)S(1)}, bf16[32,512]{1,0:T(8,128)(2,1)}, u32[]{:S(2)}) copy-start(bf16[32,512]{1,0:T(8,128)(2,1)} %param.13) | copy-start | bytes 98308
  92.2 8.7 %copy-start.1 = (bf16[1,512,4,128]{3,2,1,0:T(4,128)(2,1)S(1)}, bf16[1,512,4,128]{3,2,1,0:T(4,128)(2,1)}, u32[]{:S(2)}) copy-start(bf16[1,512,4,128]{3,2,1,0:T(4,128)(2,1)} %get-tuple-element.195) | copy-start | bytes 1572868 | tf_op jit(solution)/shard_map/while
  120.8 8.7 %copy-start.1 = (bf16[1,512,4,128]{3,2,1,0:T(4,128)(2,1)S(1)}, bf16[1,512,4,128]{3,2,1,0:T(4,128)(2,1)}, u32[]{:S(2)}) copy-start(bf16[1,512,4,128]{3,2,1,0:T(4,128)(2,1)} %get-tuple-element.195) | copy-start | bytes 1572868 | tf_op jit(solution)/shard_map/while
  150.6 8.7 %copy-start.1 = (bf16[1,512,4,128]{3,2,1,0:T(4,128)(2,1)S(1)}, bf16[1,512,4,128]{3,2,1,0:T(4,128)(2,1)}, u32[]{:S(2)}) copy-start(bf16[1,512,4,128]{3,2,1,0:T(4,128)(2,1)} %get-tuple-element.195) | copy-start | bytes 1572868 | tf_op jit(solution)/shard_map/while
  180.3 8.7 %copy-start.1 = (bf16[1,512,4,128]{3,2,1,0:T(4,128)(2,1)S(1)}, bf16[1,512,4,128]{3,2,1,0:T(4,128)(2,1)}, u32[]{:S(2)}) copy-start(bf16[1,512,4,128]{3,2,1,0:T(4,128)(2,1)} %get-tuple-element.195) | copy-start | bytes 1572868 | tf_op jit(solution)/shard_map/while
  210.1 8.7 %copy-start.1 = (bf16[1,512,4,128]{3,2,1,0:T(4,128)(2,1)S(1)}, bf16[1,512,4,128]{3,2,1,0:T(4,128)(2,1)}, u32[]{:S(2)}) copy-start(bf16[1,512,4,128]{3,2,1,0:T(4,128)(2,1)} %get-tuple-element.195) | copy-start | bytes 1572868 | tf_op jit(solution)/shard_map/while
  239.9 8.7 %copy-start.1 = (bf16[1,512,4,128]{3,2,1,0:T(4,128)(2,1)S(1)}, bf16[1,512,4,128]{3,2,1,0:T(4,128)(2,1)}, u32[]{:S(2)}) copy-start(bf16[1,512,4,128]{3,2,1,0:T(4,128)(2,1)} %get-tuple-element.195) | copy-start | bytes 1572868 | tf_op jit(solution)/shard_map/while
  269.6 8.7 %copy-start.1 = (bf16[1,512,4,128]{3,2,1,0:T(4,128)(2,1)S(1)}, bf16[1,512,4,128]{3,2,1,0:T(4,128)(2,1)}, u32[]{:S(2)}) copy-start(bf16[1,512,4,128]{3,2,1,0:T(4,128)(2,1)} %get-tuple-element.195) | copy-start | bytes 1572868 | tf_op jit(solution)/shard_map/while
  299.4 8.7 %copy-start.1 = (bf16[1,512,4,128]{3,2,1,0:T(4,128)(2,1)S(1)}, bf16[1,512,4,128]{3,2,1,0:T(4,128)(2,1)}, u32[]{:S(2)}) copy-start(bf16[1,512,4,128]{3,2,1,0:T(4,128)(2,1)} %get-tuple-element.195) | copy-start | bytes 1572868 | tf_op jit(solution)/shard_map/while
  319.6 1.0 copy-start.3
  319.6 20.6 %copy-start.7 = (bf16[32,512]{1,0:T(8,128)(2,1)S(1)}, bf16[32,512]{1,0:T(8,128)(2,1)}, u32[]{:S(2)}) copy-start(bf16[32,512]{1,0:T(8,128)(2,1)} %param.14) | copy-start | bytes 98308
  320.8 19.4 %copy-start.4 = (f32[4,2048,32]{1,2,0:T(8,128)S(1)}, f32[4,2048,32]{1,2,0:T(8,128)}, u32[]{:S(2)}) copy-start(f32[4,2048,32]{1,2,0:T(8,128)} %copy-done.3) | copy-start | bytes 3145732
  325.0 11.7 %all-to-all-start.2 = ((f32[16,1,512]{2,1,0:T(1,128)}), f32[16,1,512]{2,1,0:T(1,128)S(1)}, u32[]{:S(2)}, u32[]{:S(2)}) async-start(f32[16,1,512]{2,1,0:T(1,128)} %reshape.124), calls=%async_computation.2 | async-start | bytes 65536 | tf_op jit(solution)/shard_map/all_to_all | solution.py:112
  336.7 24.6 %all-to-all-start.1 = ((f32[16,1,512]{2,1,0:T(1,128)}), f32[16,1,512]{2,1,0:T(1,128)S(1)}, u32[]{:S(2)}, u32[]{:S(2)}) async-start(f32[16,1,512]{2,1,0:T(1,128)} %reshape.122), calls=%async_computation.1 | async-start | bytes 65536 | tf_op jit(solution)/shard_map/all_to_all | solution.py:111
  361.2 84.8 %all-to-all-start = ((f32[1,512,2048]{2,0,1:T(1,128)}), f32[1,512,2048]{2,0,1:T(1,128)}, u32[]{:S(2)}, u32[]{:S(2)}) async-start(f32[1,512,2048]{2,0,1:T(1,128)} %copy.102), calls=%async_computation | async-start | bytes 8388608 | tf_op jit(solution)/shard_map/all_to_all | solution.py:110
  368.2 157.4 %all-gather.5.cloned.1.call-start = ((), (), s32[]{:S(2)}) async-start(), calls=%async_computation.5 | async-start | bytes 2228224 | tf_op jit(solution)/shard_map/all_gather | solution.py:126
  446.0 4.3 copy-start.2
  451.2 83.9 %copy-start.6 = (bf16[256,256]{1,0:T(8,128)(2,1)S(1)}, bf16[256,256]{1,0:T(8,128)(2,1)}, u32[]{:S(2)}) copy-start(bf16[256,256]{1,0:T(8,128)(2,1)} %param.16) | copy-start | bytes 393220
  452.2 83.0 %reduce-scatter.2.cloned.1.call-start = ((), (), s32[]{:S(2)}) async-start(), calls=%async_computation.6 | async-start | bytes 393216 | tf_op jit(solution)/shard_map/reduce_scatter | solution.py:130
Sparse Core Ops, SparseCore 0:
  11.5 63.4 all-gather.2
  452.3 73.2 all-gather.4
  528.8 6.2 reduce-scatter.1
where the time goes:
time: 545 us; the launch traced here: 543 us
  waiting for transfers between devices  199 us (37%)
  matrix products  157 us (29%)
  other arithmetic  81.3 us (15%)
  local copies, waits for them, and re-layouts  76.6 us (14%)
  starting transfers between devices  14.8 us (3%)
  between operations  14.1 us (3%)
    dot_general x9, matrix products, fold_scores(): jnp.einsum('grk,kgd->grd', exps.astype(jnp.bfloat16), value_block, prefer...  88.2 us
    all_gather x1, waiting for transfers between devices, on_device(): lax.all_gather(attended, 'seq', axis=0, tiled=True)  73.4 us
    reduce_sum x9, other arithmetic, fold_scores(): running_sum = running_sum * shrink + jnp.sum(exps, axis=-1)  69.2 us
    all_to_all x1, waiting for transfers between devices, on_device(): lax.all_to_all(out_rows[None], 'seq', split_axis=1, concat_axis=0, tiled=...  67.2 us
    dot_general x8, matrix products, absorb(): jnp.einsum('grd,kgd->grk', grouped, blocks[0], preferred_element_type=jnp...  64.6 us
    all_gather x1, waiting for transfers between devices, on_device(): all_queries = lax.all_gather(query_rot, 'seq', axis=0, tiled=True)  48.6 us
    dynamic_slice x8, local copies, waits for them, and re-layouts, on_device(): lax.scan(absorb, (start_max, start_sum, start_out), (key_blocks, value_bl...  19.2 us
    another operation x1, local copies, waits for them, and re-layouts, on_device(): out_rows[None]  11 us
  transfers between devices with their start and end apart: 6, of which 5 were waited for; matrix products, arithmetic and copies ran while one was open for 9% of the time, Pallas kernels for 0%

commit v1 on v0

--- a/solution.py
+++ b/solution.py
@@ -1,8 +1,11 @@
+import functools
 import math
 
 import jax
 import jax.numpy as jnp
 from jax import lax
+from jax.experimental import pallas as pl
+from jax.experimental.pallas import tpu as pltpu
 from jax.sharding import PartitionSpec as P
 
 HD = 128
@@ -39,7 +42,7 @@
     return (new_max, running_sum, running_out)
 
 
-def on_device(
+def plain_device(
     queries, cache_keys, cache_values, new_keys, new_values, new_pos, residual, out_weight
 ):
     local_rows = queries.shape[0]
@@ -134,9 +137,380 @@
     return (attended, hidden)
 
 
+RB = 256
+KC = 2048
+SCORE_FACTOR = math.log2(math.e) / math.sqrt(HD)
+MESH = pl.DeviceIdType.MESH
+
+
+def bit_order(bits, parity):
+    order = list(range(bits - 1, -1, -1))
+    if parity:
+        order[-1], order[-2] = order[-2], order[-1]
+    return order
+
+
+def slot_owners(bits, parity):
+    order = bit_order(bits, parity)
+    return [sum(((s >> i) & 1) << b for i, b in enumerate(order)) for s in range(1 << bits)]
+
+
+def fused_kernel(
+    bits, groups, group_size, rows,
+    q_ref, kn_ref, vn_ref, kpos_ref, rinfo_ref, ck_ref, cv_ref, w_ref, res_ref,
+    att_ref, hid_ref,
+    kbuf, vbuf, wbuf, vt, s_buf, sn_buf, m_buf, qbuf, o32, stat, osend, orecv, srecv, abuf,
+    proj, total, hsend, hrecv,
+    load_sem, q_s, q_r, o_s, o_r, t_s, t_r, a_s, a_r, h_s, h_r,
+):
+    n = 1 << bits
+    keys = kbuf.shape[0]
+    kc_rows = min(KC, keys)
+    chunks = keys // kc_rows
+    blocks = n * HD // RB
+    per = RB // HD
+    me = lax.axis_index("seq")
+    core = lax.axis_index("head")
+
+    def my_slot(parity):
+        out = 0
+        for p in (0, 1):
+            slot = 0
+            for i, b in enumerate(bit_order(bits, p)):
+                slot = slot + (me // (1 << b)) % 2 * (1 << i)
+            out = out + slot * (parity if p else 1 - parity)
+        return out
+
+    def partner(parity, stage):
+        powers = [1 << bit_order(bits, p)[stage] for p in (0, 1)]
+        power = powers[0] * (1 - parity) + powers[1] * parity
+        return me + (1 - 2 * ((me // power) % 2)) * power
+
+    def remote(src, dst, send, recv, parity, stage):
+        return pltpu.make_async_remote_copy(
+            src_ref=src, dst_ref=dst, send_sem=send, recv_sem=recv,
+            device_id=(partner(parity, stage), core), device_id_type=MESH,
+        )
+
+    def gather_copy(buf, send, recv, g, stage):
+        parity = g % 2
+        size = 1 << stage
+        base = my_slot(parity) // size * size
+        part = buf.at[g, pl.ds(base, size)]
+        return remote(part, part, send.at[g, stage], recv.at[g, stage], parity, stage)
+
+    def gather_step(buf, send, recv, g, stage):
+        if stage > 0:
+            gather_copy(buf, send, recv, g, stage - 1).wait_recv()
+        if stage < bits:
+            gather_copy(buf, send, recv, g, stage).start()
+
+    def q_step(g, stage):
+        gather_step(qbuf, q_s, q_r, g, stage)
+
+    def a_step(g, stage):
+        gather_step(abuf, a_s, a_r, g, stage)
+
+    def reduce_copies(g, stage):
+        parity = g % 2
+        size = 1 << stage
+        slot = my_slot(parity)
+        other = slot // size * size + (1 - 2 * ((slot // size) % 2)) * size
+        away, land = pl.ds(other, size), pl.ds(size, size)
+        return (
+            remote(osend.at[g, away], orecv.at[g, land], o_s.at[g, stage], o_r.at[g, stage], parity, stage),
+            remote(stat.at[g, away], srecv.at[g, land], t_s.at[g, stage], t_r.at[g, stage], parity, stage),
+        )
+
+    def reduce_start(g, stage):
+        for copy in reduce_copies(g, stage):
+            copy.start()
+
+    def reduce_merge(g, stage):
+        for copy in reduce_copies(g, stage):
+            copy.wait_recv()
+        size = 1 << stage
+        kept = my_slot(g % 2) // size * size
+
+        def one(i, unused):
+            mine, theirs = stat[g, kept + i], srecv[g, size + i]
+            peak = jnp.maximum(mine[0:1], theirs[0:1])
+            w_mine, w_theirs = jnp.exp2(mine[0:1] - peak), jnp.exp2(theirs[0:1] - peak)
+            sums = mine[1:2] * w_mine + theirs[1:2] * w_theirs
+            out = o32[g, kept + i] * w_mine + orecv[g, size + i].astype(jnp.float32) * w_theirs
+            o32[g, kept + i] = out
+            osend[g, kept + i] = out.astype(jnp.bfloat16)
+            stat[g, kept + i] = jnp.concatenate(
+                [peak, sums, jnp.zeros((6, HD), jnp.float32)], axis=0
+            )
+            return 0
+
+        lax.fori_loop(0, size, one, 0)
+
+    def finish(g):
+        slot = my_slot(g % 2)
+        tile = (o32[g, slot] / stat[g, slot][1:2]).T.astype(jnp.bfloat16)
+        for h in range(group_size):
+            abuf[g, slot, :, h * HD : (h + 1) * HD] = tile[h * rows : (h + 1) * rows]
+
+    def reduce_step(g, stage):
+        reduce_merge(g, stage)
+        if stage > 0:
+            reduce_start(g, stage - 1)
+        else:
+            finish(g)
+            a_step(g, 0)
+
+    load_v = pltpu.make_async_copy(cv_ref, vbuf, load_sem.at[0])
+    load_k = pltpu.make_async_copy(ck_ref, kbuf, load_sem.at[1])
+    load_w = pltpu.make_async_copy(w_ref, wbuf, load_sem.at[2])
+    load_v.start()
+    load_k.start()
+    load_w.start()
+    barrier = pltpu.get_barrier_semaphore()
+    for b in range(bits):
+        near = me + (1 - 2 * ((me // (1 << b)) % 2)) * (1 << b)
+        pl.semaphore_signal(barrier, inc=1, device_id=(near, core), device_id_type=MESH)
+    pl.semaphore_signal(barrier, inc=1, device_id=(me, 1 - core), device_id_type=MESH)
+    pl.semaphore_wait(barrier, bits + 1)
+
+    for g in range(groups):
+        qbuf[g, my_slot(g % 2)] = q_ref[g]
+        q_step(g, 0)
+
+    load_v.wait()
+
+    def transpose_values(g):
+        def one(i, unused):
+            at = pl.ds(pl.multiple_of(i * 512, 512), 512)
+            vt[g, 0:HD, at] = vbuf[at, g * HD : (g + 1) * HD].T
+            return 0
+
+        lax.fori_loop(0, keys // 512, one, 0)
+        vt[g, 0:HD, keys : keys + HD] = vn_ref[:, g * HD : (g + 1) * HD].T
+        vt[g, HD : HD + 16, :] = jnp.ones((16, keys + HD), jnp.bfloat16)
+
+    for g in range(groups):
+        transpose_values(g)
+        q_step(0, g + 1)
+    load_k.wait()
+
+    nt = (((1,), (1,)), ((), ()))
+
+    def query_block(g, rb):
+        return qbuf[g, pl.ds(rb * per, per)].reshape(RB, HD)
+
+    def head_lanes(g):
+        return pl.ds(pl.multiple_of(g * HD, HD), HD)
+
+    def new_scores(g, rb, slot):
+        scores = lax.dot_general(
+            kn_ref[:, head_lanes(g)], query_block(g, rb), nt, preferred_element_type=jnp.float32
+        )
+        cols = pl.ds(pl.multiple_of(rb * RB, RB), RB)
+        last, first = rinfo_ref[g % 2, 0:1, cols], rinfo_ref[g % 2, 1:2, cols]
+        kpos = kpos_ref[...]
+        scores = jnp.where((kpos <= last) & (kpos >= first), scores, -1e30)
+        sn_buf[slot] = scores
+        return jnp.max(scores.reshape(rows // 8, 8, RB), axis=0)
+
+    def cache_scores(g, rb, kc, slot):
+        at = pl.ds(pl.multiple_of(kc * kc_rows, kc_rows), kc_rows)
+        scores = lax.dot_general(
+            kbuf[at, head_lanes(g)], query_block(g, rb), nt, preferred_element_type=jnp.float32
+        )
+        s_buf[slot, at, :] = scores
+        return jnp.max(scores.reshape(kc_rows // 8, 8, RB), axis=0)
+
+    m_buf[...] = lax.fori_loop(
+        0, chunks, lambda kc, m: jnp.maximum(m, cache_scores(0, 0, kc, 0)), new_scores(0, 0, 0)
+    )
+    steps = groups * blocks
+
+    def step(t, unused):
+        g, rb = t // blocks, t % blocks
+        for i, stage in ((0, 1), (1, 2), (3, 3), (7, 4)):
+            pl.when((rb == i) & (g < groups - 1))(functools.partial(q_step, g + 1, stage))
+        pl.when((rb == 0) & (g > 0))(functools.partial(reduce_start, g - 1, bits - 1))
+        for i, stage in ((3, 3), (5, 2), (6, 1), (7, 0)):
+            pl.when((rb == i) & (g > 0))(functools.partial(reduce_step, g - 1, stage))
+        for i, stage in ((0, 1), (1, 2), (3, 3), (6, 4)):
+            pl.when((rb == i) & (g > 1))(functools.partial(a_step, g - 2, stage))
+
+        now, later = t % 2, (t + 1) % 2
+        after = jnp.minimum(t + 1, steps - 1)
+        g2, rb2 = after // blocks, after % blocks
+        peak = jnp.max(m_buf[...], axis=0, keepdims=True) * SCORE_FACTOR
+        m0 = new_scores(g2, rb2, later)
+        p_new = jnp.exp2(sn_buf[now] * SCORE_FACTOR - peak).astype(jnp.bfloat16)
+        p_new = jnp.concatenate([p_new, jnp.zeros((HD - rows, RB), jnp.bfloat16)], axis=0)
+        acc = jnp.dot(vt[g, :, keys : keys + HD], p_new, preferred_element_type=jnp.float32)
+
+        def inner(kc, carry):
+            m, acc = carry
+            at = pl.ds(pl.multiple_of(kc * kc_rows, kc_rows), kc_rows)
+            p = jnp.exp2(s_buf[now, at, :] * SCORE_FACTOR - peak).astype(jnp.bfloat16)
+            acc = acc + jnp.dot(vt[g, :, at], p, preferred_element_type=jnp.float32)
+            return jnp.maximum(m, cache_scores(g2, rb2, kc, later)), acc
+
+        m, acc = lax.fori_loop(0, chunks, inner, (m0, acc))
+        m_buf[...] = m
+        for i in range(per):
+            lanes = slice(i * HD, (i + 1) * HD)
+            out = acc[0:HD, lanes]
+            o32[g, rb * per + i] = out
+            osend[g, rb * per + i] = out.astype(jnp.bfloat16)
+            stat[g, rb * per + i] = jnp.concatenate(
+                [peak[:, lanes], acc[HD : HD + 1, lanes], jnp.zeros((6, HD), jnp.float32)], axis=0
+            )
+        return 0
+
+    lax.fori_loop(0, steps, step, 0)
+
+    def project(g):
+        part = jnp.dot(
+            abuf[g].reshape(n * rows, group_size * HD),
+            wbuf[g * group_size * HD : (g + 1) * group_size * HD, :],
+            preferred_element_type=jnp.float32,
+        )
+        proj[g % 2] = part if g < 2 else proj[g % 2] + part
+
+    last = groups - 1
+    reduce_start(last, bits - 1)
+    a_step(last - 1, 1)
+    load_w.wait()
+    for g in range(last - 1):
+        project(g)
+    a_step(last - 1, 2)
+    a_step(last - 1, 3)
+    reduce_step(last, 3)
+    reduce_step(last, 2)
+    reduce_step(last, 1)
+    reduce_step(last, 0)
+    a_step(last - 1, 4)
+    a_step(last, 1)
+    project(last - 1)
+    for g in range(groups):
+        att_ref[:, g * group_size * HD : (g + 1) * group_size * HD] = abuf[g, my_slot(g % 2)]
+    a_step(last, 2)
+    a_step(last, 3)
+    a_step(last, 4)
+    project(last)
+    even, odd = slot_owners(bits, 0), slot_owners(bits, 1)
+    for owner in range(n):
+        se, so = even.index(owner), odd.index(owner)
+        tile = proj[0, se * rows : (se + 1) * rows] + proj[1, so * rows : (so + 1) * rows]
+        half, at = owner // (n // 2), owner % (n // 2) * rows
+        total[half, at : at + rows] = tile
+        hsend[half, at : at + rows] = tile.astype(jnp.bfloat16)
+    swap = pltpu.make_async_remote_copy(
+        src_ref=hsend.at[1 - core], dst_ref=hrecv, send_sem=h_s, recv_sem=h_r,
+        device_id=(me, 1 - core), device_id_type=MESH,
+    )
+    swap.start()
+    swap.wait_recv()
+    summed = total[core] + hrecv[...].astype(jnp.float32)
+    hid_ref[...] = (res_ref[...].astype(jnp.float32) + summed).astype(jnp.bfloat16)
+    swap.wait_send()
+
+    def drain(g, unused):
+        for stage in range(bits):
+            gather_copy(qbuf, q_s, q_r, g, stage).wait_send()
+            gather_copy(abuf, a_s, a_r, g, stage).wait_send()
+            for copy in reduce_copies(g, stage):
+                copy.wait_send()
+        return 0
+
+    lax.fori_loop(0, groups, drain, 0)
+
+
+def fused_device(
+    n, queries, cache_keys, cache_values, new_keys, new_values, new_pos, residual, out_weight
+):
+    bits = n.bit_length() - 1
+    rows = queries.shape[0]
+    keys = cache_keys.shape[0]
+    groups = cache_keys.shape[1] // HD
+    group_size = queries.shape[1] // cache_keys.shape[1]
+    row_start = lax.axis_index("seq") * rows
+    own_pos = lax.dynamic_slice_in_dim(new_pos, row_start, rows)
+    own_offsets = own_pos % TURN
+    q_rot = rotate(
+        queries.astype(jnp.float32).reshape(rows, groups * group_size, HD), own_offsets
+    ).astype(jnp.bfloat16)
+    q_rot = (
+        q_rot.reshape(rows, groups, group_size, HD)
+        .transpose(1, 2, 0, 3)
+        .reshape(groups, group_size * rows, HD)
+    )
+    k_rot = rotate(
+        new_keys.astype(jnp.float32).reshape(rows, groups, HD), own_offsets
+    ).astype(jnp.bfloat16).reshape(rows, groups * HD)
+    v_new = jnp.pad(new_values, ((0, HD - rows), (0, 0)))
+    kpos = jnp.broadcast_to(own_pos[:, None], (rows, RB))
+    infos = []
+    for parity in (0, 1):
+        table = new_pos.reshape(n, rows)[jnp.array(slot_owners(bits, parity), jnp.int32)]
+        table = jnp.broadcast_to(table[:, None, :], (n, group_size, rows)).reshape(-1)
+        infos.append(jnp.stack([table, table // TURN * TURN]))
+    rinfo = jnp.stack(infos)
+    bf, f32 = jnp.bfloat16, jnp.float32
+    vmem, hbm = pl.BlockSpec(memory_space=pltpu.VMEM), pl.BlockSpec(memory_space=pl.ANY)
+    sems = pltpu.SemaphoreType.DMA((groups, bits))
+    width = out_weight.shape[1]
+    half = n * rows // 2
+    return pl.pallas_call(
+        functools.partial(fused_kernel, bits, groups, group_size, rows),
+        out_shape=(
+            jax.ShapeDtypeStruct(queries.shape, bf),
+            jax.ShapeDtypeStruct(residual.shape, bf),
+        ),
+        in_specs=[vmem] * 5 + [hbm] * 3 + [vmem],
+        out_specs=(vmem, vmem),
+        scratch_shapes=[
+            pltpu.VMEM(cache_keys.shape, bf),
+            pltpu.VMEM(cache_values.shape, bf),
+            pltpu.VMEM(out_weight.shape, bf),
+            pltpu.VMEM((groups, HD + 16, keys + HD), bf),
+            pltpu.VMEM((2, keys, RB), f32),
+            pltpu.VMEM((2, rows, RB), f32),
+            pltpu.VMEM((8, RB), f32),
+            pltpu.VMEM((groups, n, HD, HD), bf),
+            pltpu.VMEM((groups, n, HD, HD), f32),
+            pltpu.VMEM((groups, n, 8, HD), f32),
+            pltpu.VMEM((groups, n, HD, HD), bf),
+            pltpu.VMEM((groups, n, HD, HD), bf),
+            pltpu.VMEM((groups, n, 8, HD), f32),
+            pltpu.VMEM((groups, n, rows, group_size * HD), bf),
+            pltpu.VMEM((2, n * rows, width), f32),
+            pltpu.VMEM((2, half, width), f32),
+            pltpu.VMEM((2, half, width), bf),
+            pltpu.VMEM((half, width), bf),
+            pltpu.SemaphoreType.DMA((3,)),
+            sems, sems, sems, sems, sems, sems, sems, sems,
+            pltpu.SemaphoreType.DMA,
+            pltpu.SemaphoreType.DMA,
+        ],
+        compiler_params=pltpu.CompilerParams(
+            collective_id=0, has_side_effects=True, vmem_limit_bytes=60 * 2**20
+        ),
+    )(q_rot, k_rot, v_new, kpos, rinfo, cache_keys, cache_values, out_weight, residual)
+
+
+def on_device(n, *arrays):
+    queries, cache_keys = arrays[0], arrays[1]
+    rows, keys = queries.shape[0], cache_keys.shape[0]
+    groups = cache_keys.shape[1] // HD
+    group_size = queries.shape[1] // cache_keys.shape[1]
+    fits = n == 16 and groups == 4 and rows == 32 and group_size * rows == HD and keys % KC == 0
+    if fits and keys == 4096:
+        return fused_device(n, *arrays)
+    return plain_device(*arrays)
+
+
 def solution(mesh):
     return jax.shard_map(
-        on_device,
+        functools.partial(on_device, mesh.shape["seq"]),
         mesh=mesh,
         in_specs=(
             P("seq", "head"),

time: 545 us -> 167 us (0.31)
  waiting for transfers between devices: 199 us -> 0 us
  matrix products: 157 us -> 0 us
  Pallas kernels: 0 us -> 155 us
  other arithmetic: 81.3 us -> 4.46 us
  local copies, waits for them, and re-layouts: 76.6 us -> 7.27 us
  starting transfers between devices: 14.8 us -> 0 us
  between operations: 14.1 us -> 0.82 us
    dot_general x19 -> x0, matrix products: 157 us -> none  [the longest x9 88.2 us: fold_scores(): jnp.einsum('grk,kgd->grd', exps.astype(jnp.bfloat16), value_block, prefer...]
    pallas_call x0 -> x1, Pallas kernels: none -> 155 us  [fused_device(): pl.pallas_call(functools.partial(fused_kernel, bits, groups, group_size,...]
    all_gather x2 -> x0, waiting for transfers between devices: 122 us -> none  [the longest x1 73.4 us: on_device(): lax.all_gather(attended, 'seq', axis=0, tiled=True)]
    all_to_all x3 -> x0, waiting for transfers between devices: 71 us -> none  [the longest x1 67.2 us: on_device(): lax.all_to_all(out_rows[None], 'seq', split_axis=1, concat_axis=0, tiled=...]
    reduce_sum x11 -> x0, other arithmetic: 70.2 us -> none  [the longest x9 69.2 us: fold_scores(): running_sum = running_sum * shrink + jnp.sum(exps, axis=-1)]
    reshape x7 -> x3, local copies, waits for them, and re-layouts: 28 us -> 1.22 us  [the longest x1 1.12 us: fused_device(): queries.astype(jnp.float32).reshape(rows, groups * group_size, HD)]
    dynamic_slice x9 -> x0, local copies, waits for them, and re-layouts: 19.2 us -> none  [the longest x8 19.2 us: on_device(): lax.scan(absorb, (start_max, start_sum, start_out), (key_blocks, value_bl...]
    all_to_all x3 -> x0, starting transfers between devices: 14.7 us -> none  [the longest x1 6.93 us: on_device(): lax.all_to_all(out_rows[None], 'seq', split_axis=1, concat_axis=0, tiled=...]
  transfers between devices with their start and end apart: 6 -> 0, of which waited for: 5 -> 0; matrix products, arithmetic and copies ran while one was open for 9% -> 0% of each run, Pallas kernels for 0% -> 0%
where the time goes in v1:
time: 167 us
  Pallas kernels  155 us (93%)
  local copies, waits for them, and re-layouts  7.27 us (4%)
  other arithmetic  4.46 us (3%)
    pallas_call x1, Pallas kernels, fused_device(): pl.pallas_call(functools.partial(fused_kernel, bits, groups, group_size,...  155 us

profile of v1, /device:TPU:0, one launch (start us, length us, event | category | flops | bytes accessed | tf_op | source)
XLA Modules:
  0.0 167.1 jit_solution(13781734872056071143)
XLA Ops:
  0.6 0.0 copy-start.4
  0.6 0.0 copy-start.3
  0.7 0.0 copy-start.2
  0.7 0.0 copy-start
  0.7 0.0 copy-start.1
  0.7 0.8 fusion.5
  1.5 0.1 multiply_cosine_fusion
  1.7 0.1 pad_maximum_fusion
  1.7 0.9 convert_bitcast_fusion
  2.7 0.1 slice_negate_fusion
  2.9 0.1 copy.13
  3.0 0.1 copy.14
  3.1 1.1 reshape.187
  4.2 0.8 fusion.1
  5.0 0.0 copy-done
  5.0 0.1 slice_negate_fusion.1
  5.1 0.1 maximum_multiply_fusion.1
  5.2 0.6 fusion.2.kn_ref
  5.9 0.0 copy-done.2
  5.9 0.1 reshape.191
  5.9 0.0 copy-done.4
  6.0 0.6 gather_fusion.1
  6.5 0.1 stack_reshape.7
  6.7 0.0 copy-done.3
  6.7 0.6 gather_fusion
  7.3 0.1 stack_reshape.6
  7.5 0.6 pad_add_fusion.rinfo_ref
  8.1 0.7 broadcast_in_dim.10.kpos_ref
  8.7 0.0 copy-done.1
  8.7 0.7 pad.4.vn_ref
  9.4 154.5 %shard_map.113 = (bf16[32,2048]{1,0:T(8,128)(2,1)}, bf16[256,256]{1,0:T(8,128)(2,1)}) custom-call(bf16[4,128,128]{2,1,0:T(8,128)(2,1)} %bitcast.25, bf16[32,512]{1,0:T(8,128)(2,1)} %fusion.2.kn_ref, bf16[128,512]{1,0:T(8,128)(2,1)} %pad.4.vn_ref, s32[32,256]{1,0:T(8,128)} %broadcast_in_dim.10.kpos_ref, s32[2,2,2048]{2,1,0:T(2,128)} %pad_add_fusion.rinfo_ref, ...), custom_call_target="tpu_custom_call" | custom-call | tf_op jit(solution)/shard_map/pallas_call | solution.py:462
  163.9 1.6 copy.25
  165.5 1.6 copy.26
  (11 shorter events, 0.2 us)
Async XLA Ops:
  0.6 5.3 %copy-start.4 = (s32[16]{0:T(128)S(1)}, s32[16]{0:T(128)}, u32[]{:S(2)}) copy-start(s32[16]{0:T(128)} %constant.71) | copy-start | bytes 196
  0.6 6.0 %copy-start.3 = (s32[16]{0:T(128)S(1)}, s32[16]{0:T(128)}, u32[]{:S(2)}) copy-start(s32[16]{0:T(128)} %constant.70) | copy-start | bytes 196
  0.7 5.2 %copy-start.2 = (s32[512]{0:T(512)S(1)}, s32[512]{0:T(512)}, u32[]{:S(2)}) copy-start(s32[512]{0:T(512)} %param.15) | copy-start | bytes 6148
  0.7 4.3 %copy-start = (bf16[32,512]{1,0:T(8,128)(2,1)S(1)}, bf16[32,512]{1,0:T(8,128)(2,1)}, u32[]{:S(2)}) copy-start(bf16[32,512]{1,0:T(8,128)(2,1)} %param.13) | copy-start | bytes 98308
  0.7 8.1 %copy-start.1 = (bf16[32,512]{1,0:T(8,128)(2,1)S(1)}, bf16[32,512]{1,0:T(8,128)(2,1)}, u32[]{:S(2)}) copy-start(bf16[32,512]{1,0:T(8,128)(2,1)} %param.14) | copy-start | bytes 98308

commit v2 on v1

--- a/solution.py
+++ b/solution.py
@@ -157,11 +157,11 @@
 
 def fused_kernel(
     bits, groups, group_size, rows,
-    q_ref, kn_ref, vn_ref, kpos_ref, rinfo_ref, ck_ref, cv_ref, w_ref, res_ref,
+    q_ref, kn_ref, vn_ref, trig_ref, kpos_ref, rinfo_ref, ck_ref, cv_ref, w_ref, res_ref,
     att_ref, hid_ref,
     kbuf, vbuf, wbuf, vt, s_buf, sn_buf, m_buf, qbuf, o32, stat, osend, orecv, srecv, abuf,
     proj, total, hsend, hrecv,
-    load_sem, q_s, q_r, o_s, o_r, t_s, t_r, a_s, a_r, h_s, h_r,
+    knew, load_sem, q_s, q_r, o_s, o_r, t_s, t_r, a_s, a_r, h_s, h_r, d_s, d_r,
 ):
     n = 1 << bits
     keys = kbuf.shape[0]
@@ -261,6 +261,53 @@
             finish(g)
             a_step(g, 0)
 
+    def flip(mask):
+        out = me
+        for b in range(bits):
+            if mask >> b & 1:
+                out = out + (1 - 2 * ((me // (1 << b)) % 2)) * (1 << b)
+        return out
+
+    def flip_slot(slot, delta):
+        for b in range(bits):
+            if delta >> b & 1:
+                slot = slot + (1 - 2 * ((slot // (1 << b)) % 2)) * (1 << b)
+        return slot
+
+    def device_at(g, delta):
+        order = bit_order(bits, g % 2)
+        return flip(sum(1 << order[b] for b in range(bits) if delta >> b & 1))
+
+    def direct(src, dst, kind, g, delta, i):
+        return pltpu.make_async_remote_copy(
+            src_ref=src, dst_ref=dst, send_sem=d_s.at[kind, i], recv_sem=d_r.at[kind, i],
+            device_id=(device_at(g, delta), core), device_id_type=MESH,
+        )
+
+    def spread_copies(g, phase):
+        size = 1 if phase == 0 else 4
+        part = abuf.at[g, pl.ds(my_slot(g % 2) // size * size, size)]
+        return [direct(part, part, phase, g, i * size, i - 1) for i in (1, 2, 3)]
+
+    def last_copies(g):
+        out = []
+        slot = my_slot(g % 2)
+        for i in (1, 2, 3):
+            away = flip_slot(slot, i)
+            out.append(direct(osend.at[g, away], orecv.at[g, i], 2, g, i, i - 1))
+            out.append(direct(stat.at[g, away], srecv.at[g, i], 3, g, i, i - 1))
+        return out
+
+    def last_merge(g):
+        slot = my_slot(g % 2)
+        stats = [stat[g, slot]] + [srecv[g, i] for i in (1, 2, 3)]
+        peak = functools.reduce(jnp.maximum, [x[0:1] for x in stats])
+        weights = [jnp.exp2(x[0:1] - peak) for x in stats]
+        outs = [o32[g, slot]] + [orecv[g, i].astype(jnp.float32) for i in (1, 2, 3)]
+        sums = sum(x[1:2] * w for x, w in zip(stats, weights))
+        o32[g, slot] = sum(o * w for o, w in zip(outs, weights))
+        stat[g, slot] = jnp.concatenate([peak, sums, jnp.zeros((6, HD), jnp.float32)], axis=0)
+
     load_v = pltpu.make_async_copy(cv_ref, vbuf, load_sem.at[0])
     load_k = pltpu.make_async_copy(ck_ref, kbuf, load_sem.at[1])
     load_w = pltpu.make_async_copy(w_ref, wbuf, load_sem.at[2])
@@ -268,15 +315,30 @@
     load_k.start()
     load_w.start()
     barrier = pltpu.get_barrier_semaphore()
-    for b in range(bits):
-        near = me + (1 - 2 * ((me // (1 << b)) % 2)) * (1 << b)
-        pl.semaphore_signal(barrier, inc=1, device_id=(near, core), device_id_type=MESH)
+    masks = [1 << b for b in range(bits)] + [3, 3 << (bits - 2)]
+    for mask in masks:
+        pl.semaphore_signal(barrier, inc=1, device_id=(flip(mask), core), device_id_type=MESH)
     pl.semaphore_signal(barrier, inc=1, device_id=(me, 1 - core), device_id_type=MESH)
-    pl.semaphore_wait(barrier, bits + 1)
+
+    def barrier_wait():
+        pl.semaphore_wait(barrier, len(masks) + 1)
+
+    cosine, sine = trig_ref[0], trig_ref[1]
+
+    def turned(block):
+        x = block.astype(jnp.float32)
+        return (x * cosine + pltpu.roll(x, HD // 2, 1) * sine).astype(jnp.bfloat16)
 
     for g in range(groups):
-        qbuf[g, my_slot(g % 2)] = q_ref[g]
+        slot = my_slot(g % 2)
+        for h in range(group_size):
+            at = (g * group_size + h) * HD
+            qbuf[g, slot, h * rows : (h + 1) * rows] = turned(q_ref[:, at : at + HD])
+    barrier_wait()
+    for g in range(groups):
         q_step(g, 0)
+    for g in range(groups):
+        knew[:, g * HD : (g + 1) * HD] = turned(kn_ref[:, g * HD : (g + 1) * HD])
 
     load_v.wait()
 
@@ -287,12 +349,16 @@
             return 0
 
         lax.fori_loop(0, keys // 512, one, 0)
-        vt[g, 0:HD, keys : keys + HD] = vn_ref[:, g * HD : (g + 1) * HD].T
+        fresh = jnp.concatenate(
+            [vn_ref[:, g * HD : (g + 1) * HD], jnp.zeros((HD - rows, HD), jnp.bfloat16)], axis=0
+        )
+        vt[g, 0:HD, keys : keys + HD] = fresh.T
         vt[g, HD : HD + 16, :] = jnp.ones((16, keys + HD), jnp.bfloat16)
 
-    for g in range(groups):
+    transpose_values(0)
+    q_step(0, 1)
+    for g in range(1, groups):
         transpose_values(g)
-        q_step(0, g + 1)
     load_k.wait()
 
     nt = (((1,), (1,)), ((), ()))
@@ -305,10 +371,11 @@
 
     def new_scores(g, rb, slot):
         scores = lax.dot_general(
-            kn_ref[:, head_lanes(g)], query_block(g, rb), nt, preferred_element_type=jnp.float32
+            knew[:, head_lanes(g)], query_block(g, rb), nt, preferred_element_type=jnp.float32
         )
         cols = pl.ds(pl.multiple_of(rb * RB, RB), RB)
-        last, first = rinfo_ref[g % 2, 0:1, cols], rinfo_ref[g % 2, 1:2, cols]
+        last = rinfo_ref[g % 2, :, cols]
+        first = last - (last & (TURN - 1))
         kpos = kpos_ref[...]
         scores = jnp.where((kpos <= last) & (kpos >= first), scores, -1e30)
         sn_buf[slot] = scores
@@ -322,24 +389,47 @@
         s_buf[slot, at, :] = scores
         return jnp.max(scores.reshape(kc_rows // 8, 8, RB), axis=0)
 
+    levels = blocks.bit_length() - 1
+
+    def block_at(g, j):
+        first = 1 - jnp.minimum(g, 1)
+        mine = my_slot(g % 2) // per
+        out = 0
+        for b in range(levels):
+            same = (mine // (1 << b) + j // (1 << b) + 1 - first) % 2
+            out = out + same * (1 << b)
+        return out
+
+    start = block_at(0, 0)
     m_buf[...] = lax.fori_loop(
-        0, chunks, lambda kc, m: jnp.maximum(m, cache_scores(0, 0, kc, 0)), new_scores(0, 0, 0)
+        0, chunks, lambda kc, m: jnp.maximum(m, cache_scores(0, start, kc, 0)),
+        new_scores(0, start, 0),
     )
     steps = groups * blocks
 
     def step(t, unused):
-        g, rb = t // blocks, t % blocks
+        g, j = t // blocks, t % blocks
+        for i, stage in ((0, 2), (1, 3), (3, 4)):
+            pl.when(t == i)(functools.partial(q_step, 0, stage))
         for i, stage in ((0, 1), (1, 2), (3, 3), (7, 4)):
-            pl.when((rb == i) & (g < groups - 1))(functools.partial(q_step, g + 1, stage))
-        pl.when((rb == 0) & (g > 0))(functools.partial(reduce_start, g - 1, bits - 1))
+            pl.when((j == i) & (g < groups - 1))(functools.partial(q_step, g + 1, stage))
+        pl.when((j == 4) & (g > 0))(functools.partial(reduce_start, g, bits - 1))
+        pl.when(t == blocks)(functools.partial(reduce_start, 0, bits - 1))
         for i, stage in ((3, 3), (5, 2), (6, 1), (7, 0)):
-            pl.when((rb == i) & (g > 0))(functools.partial(reduce_step, g - 1, stage))
-        for i, stage in ((0, 1), (1, 2), (3, 3), (6, 4)):
-            pl.when((rb == i) & (g > 1))(functools.partial(a_step, g - 2, stage))
+            pl.when((j == i) & (g == 1))(functools.partial(reduce_step, 0, stage))
+        for i, stage in ((0, 3), (2, 2), (3, 1), (4, 0)):
+            pl.when((j == i) & (g > 1))(functools.partial(reduce_step, g - 1, stage))
+        for i, stage in ((0, 1), (1, 2), (2, 3), (5, 4)):
+            pl.when((j == i) & (g == 2))(functools.partial(a_step, 0, stage))
+        for i, stage in ((5, 1), (6, 2), (7, 3)):
+            pl.when((j == i) & (g > 1))(functools.partial(a_step, g - 1, stage))
+        pl.when((j == 2) & (g > 2))(functools.partial(a_step, g - 2, 4))
+        rb = block_at(g, j)
 
         now, later = t % 2, (t + 1) % 2
         after = jnp.minimum(t + 1, steps - 1)
-        g2, rb2 = after // blocks, after % blocks
+        g2 = after // blocks
+        rb2 = block_at(g2, after % blocks)
         peak = jnp.max(m_buf[...], axis=0, keepdims=True) * SCORE_FACTOR
         m0 = new_scores(g2, rb2, later)
         p_new = jnp.exp2(sn_buf[now] * SCORE_FACTOR - peak).astype(jnp.bfloat16)
@@ -376,25 +466,29 @@
         proj[g % 2] = part if g < 2 else proj[g % 2] + part
 
     last = groups - 1
-    reduce_start(last, bits - 1)
-    a_step(last - 1, 1)
+    reduce_step(last, 3)
     load_w.wait()
     for g in range(last - 1):
         project(g)
-    a_step(last - 1, 2)
-    a_step(last - 1, 3)
-    reduce_step(last, 3)
-    reduce_step(last, 2)
-    reduce_step(last, 1)
-    reduce_step(last, 0)
+    reduce_merge(last, 2)
+    for copy in last_copies(last):
+        copy.start()
     a_step(last - 1, 4)
-    a_step(last, 1)
     project(last - 1)
+    for copy in last_copies(last):
+        copy.wait_recv()
+    last_merge(last)
+    finish(last)
+    for copy in spread_copies(last, 0):
+        copy.start()
     for g in range(groups):
         att_ref[:, g * group_size * HD : (g + 1) * group_size * HD] = abuf[g, my_slot(g % 2)]
-    a_step(last, 2)
-    a_step(last, 3)
-    a_step(last, 4)
+    for copy in spread_copies(last, 0):
+        copy.wait_recv()
+    for copy in spread_copies(last, 1):
+        copy.start()
+    for copy in spread_copies(last, 1):
+        copy.wait_recv()
     project(last)
     even, odd = slot_owners(bits, 0), slot_owners(bits, 1)
     for owner in range(n):
@@ -416,12 +510,23 @@
     def drain(g, unused):
         for stage in range(bits):
             gather_copy(qbuf, q_s, q_r, g, stage).wait_send()
-            gather_copy(abuf, a_s, a_r, g, stage).wait_send()
+        for stage in (2, 3):
             for copy in reduce_copies(g, stage):
                 copy.wait_send()
         return 0
 
+    def drain_rest(g, unused):
+        for stage in range(bits):
+            gather_copy(abuf, a_s, a_r, g, stage).wait_send()
+        for stage in (0, 1):
+            for copy in reduce_copies(g, stage):
+                copy.wait_send()
+        return 0
+
     lax.fori_loop(0, groups, drain, 0)
+    lax.fori_loop(0, last, drain_rest, 0)
+    for copy in last_copies(last) + spread_copies(last, 0) + spread_copies(last, 1):
+        copy.wait_send()
 
 
 def fused_device(
@@ -434,25 +539,19 @@
     group_size = queries.shape[1] // cache_keys.shape[1]
     row_start = lax.axis_index("seq") * rows
     own_pos = lax.dynamic_slice_in_dim(new_pos, row_start, rows)
-    own_offsets = own_pos % TURN
-    q_rot = rotate(
-        queries.astype(jnp.float32).reshape(rows, groups * group_size, HD), own_offsets
-    ).astype(jnp.bfloat16)
-    q_rot = (
-        q_rot.reshape(rows, groups, group_size, HD)
-        .transpose(1, 2, 0, 3)
-        .reshape(groups, group_size * rows, HD)
-    )
-    k_rot = rotate(
-        new_keys.astype(jnp.float32).reshape(rows, groups, HD), own_offsets
-    ).astype(jnp.bfloat16).reshape(rows, groups * HD)
-    v_new = jnp.pad(new_values, ((0, HD - rows), (0, 0)))
+    frequency = jnp.exp(
+        (jnp.arange(HD, dtype=jnp.int32) % (HD // 2)).astype(jnp.float32)
+        * (-2.0 * math.log(rope_base) / HD)
+    )
+    angles = (own_pos % TURN).astype(jnp.float32)[:, None] * frequency[None, :]
+    sign = jnp.where(jnp.arange(HD) < HD // 2, -1.0, 1.0)
+    trig = jnp.stack([jnp.cos(angles), jnp.sin(angles) * sign])
     kpos = jnp.broadcast_to(own_pos[:, None], (rows, RB))
     infos = []
     for parity in (0, 1):
-        table = new_pos.reshape(n, rows)[jnp.array(slot_owners(bits, parity), jnp.int32)]
-        table = jnp.broadcast_to(table[:, None, :], (n, group_size, rows)).reshape(-1)
-        infos.append(jnp.stack([table, table // TURN * TURN]))
+        axes = [bits - 1 - b for b in reversed(bit_order(bits, parity))]
+        table = new_pos.reshape((2,) * bits + (rows,)).transpose(*axes, bits).reshape(n, 1, rows)
+        infos.append(jnp.broadcast_to(table, (n, group_size, rows)).reshape(1, -1))
     rinfo = jnp.stack(infos)
     bf, f32 = jnp.bfloat16, jnp.float32
     vmem, hbm = pl.BlockSpec(memory_space=pltpu.VMEM), pl.BlockSpec(memory_space=pl.ANY)
@@ -465,7 +564,7 @@
             jax.ShapeDtypeStruct(queries.shape, bf),
             jax.ShapeDtypeStruct(residual.shape, bf),
         ),
-        in_specs=[vmem] * 5 + [hbm] * 3 + [vmem],
+        in_specs=[vmem] * 6 + [hbm] * 3 + [vmem],
         out_specs=(vmem, vmem),
         scratch_shapes=[
             pltpu.VMEM(cache_keys.shape, bf),
@@ -486,15 +585,21 @@
             pltpu.VMEM((2, half, width), f32),
             pltpu.VMEM((2, half, width), bf),
             pltpu.VMEM((half, width), bf),
+            pltpu.VMEM(new_keys.shape, bf),
             pltpu.SemaphoreType.DMA((3,)),
             sems, sems, sems, sems, sems, sems, sems, sems,
             pltpu.SemaphoreType.DMA,
             pltpu.SemaphoreType.DMA,
+            pltpu.SemaphoreType.DMA((4, 3)),
+            pltpu.SemaphoreType.DMA((4, 3)),
         ],
         compiler_params=pltpu.CompilerParams(
             collective_id=0, has_side_effects=True, vmem_limit_bytes=60 * 2**20
         ),
-    )(q_rot, k_rot, v_new, kpos, rinfo, cache_keys, cache_values, out_weight, residual)
+    )(
+        queries, new_keys, new_values, trig, kpos, rinfo,
+        cache_keys, cache_values, out_weight, residual,
+    )
 
 
 def on_device(n, *arrays):

time: 167 us -> 149 us (0.89)
  Pallas kernels: 155 us -> 141 us
  local copies, waits for them, and re-layouts: 7.27 us -> 4.8 us
  other arithmetic: 4.46 us -> 2.14 us
    pallas_call x1, Pallas kernels: 155 us -> 141 us  [fused_device(): pl.pallas_call(functools.partial(fused_kernel, bits, groups, group_size,...]
where the time goes in v2:
time: 149 us; the launch traced here: 148 us
  Pallas kernels  141 us (95%)
  local copies, waits for them, and re-layouts  4.8 us (3%)
  other arithmetic  2.14 us (1%)
    pallas_call x1, Pallas kernels, fused_device(): pl.pallas_call(functools.partial(fused_kernel, bits, groups, group_size,...  141 us
    unnamed x2, local copies, waits for them, and re-layouts  3.14 us

profile of v2, /device:TPU:0, one launch (start us, length us, event | category | flops | bytes accessed | tf_op | source)
XLA Modules:
  0.0 148.3 jit_solution(1424267248171644633)
XLA Ops:
  0.6 0.8 fusion.1
  1.4 0.8 reshape.139
  2.2 0.1 stack_reshape.7
  2.3 0.1 stack_reshape.6
  2.4 0.6 pad_add_fusion.rinfo_ref
  3.0 0.1 multiply_cosine_fusion
  3.2 0.6 pad_maximum_fusion.trig_ref
  3.8 0.7 broadcast_in_dim.33.kpos_ref
  4.5 140.7 %shard_map.95 = (bf16[32,2048]{1,0:T(8,128)(2,1)}, bf16[256,256]{1,0:T(8,128)(2,1)}) custom-call(bf16[32,2048]{1,0:T(8,128)(2,1)} %q_ref.1, bf16[32,512]{1,0:T(8,128)(2,1)} %kn_ref.1, bf16[32,512]{1,0:T(8,128)(2,1)} %vn_ref.1, f32[2,32,128]{2,1,0:T(8,128)} %pad_maximum_fusion.trig_ref, s32[32,256]{1,0:T(8,128)} %broadcast_in_dim.33.kpos_ref, ...), custom_call_target="tpu_custom_call" | custom-call | tf_op jit(solution)/shard_map/pallas_call | solution.py:561
  145.1 1.6 %copy.15 = bf16[32,2048]{1,0:T(8,128)(2,1)} copy(bf16[32,2048]{1,0:T(8,128)(2,1)} %get-tuple-element.10) | data formatting | bytes 262144
  146.7 1.6 %copy.16 = bf16[256,256]{1,0:T(8,128)(2,1)} copy(bf16[256,256]{1,0:T(8,128)(2,1)} %get-tuple-element.11) | data formatting | bytes 262144
  (5 shorter events, 0.0 us)

commit v3 on v2

--- a/solution.py
+++ b/solution.py
@@ -253,14 +253,6 @@
         for h in range(group_size):
             abuf[g, slot, :, h * HD : (h + 1) * HD] = tile[h * rows : (h + 1) * rows]
 
-    def reduce_step(g, stage):
-        reduce_merge(g, stage)
-        if stage > 0:
-            reduce_start(g, stage - 1)
-        else:
-            finish(g)
-            a_step(g, 0)
-
     def flip(mask):
         out = me
         for b in range(bits):
@@ -275,12 +267,12 @@
         return slot
 
     def device_at(g, delta):
-        order = bit_order(bits, g % 2)
+        order = bit_order(bits, 0 if delta < 4 else g % 2)
         return flip(sum(1 << order[b] for b in range(bits) if delta >> b & 1))
 
     def direct(src, dst, kind, g, delta, i):
         return pltpu.make_async_remote_copy(
-            src_ref=src, dst_ref=dst, send_sem=d_s.at[kind, i], recv_sem=d_r.at[kind, i],
+            src_ref=src, dst_ref=dst, send_sem=d_s.at[g, kind, i], recv_sem=d_r.at[g, kind, i],
             device_id=(device_at(g, delta), core), device_id_type=MESH,
         )
 
@@ -307,6 +299,43 @@
         sums = sum(x[1:2] * w for x, w in zip(stats, weights))
         o32[g, slot] = sum(o * w for o, w in zip(outs, weights))
         stat[g, slot] = jnp.concatenate([peak, sums, jnp.zeros((6, HD), jnp.float32)], axis=0)
+
+    def start_all(copies):
+        for copy in copies:
+            copy.start()
+
+    def reduce_next(g):
+        reduce_merge(g, 3)
+        reduce_start(g, 2)
+
+    def reduce_direct(g):
+        reduce_merge(g, 2)
+        start_all(last_copies(g))
+
+    def reduce_end(g):
+        for copy in last_copies(g):
+            copy.wait_recv()
+        last_merge(g)
+        finish(g)
+        start_all(spread_copies(g, 0))
+
+    def a_second(g):
+        for copy in spread_copies(g, 0):
+            copy.wait_recv()
+        gather_copy(abuf, a_s, a_r, g, 2).start()
+
+    events = (
+        (0, q_step, 0, 2), (0, q_step, 1, 1), (1, q_step, 0, 3), (2, q_step, 1, 2),
+        (3, q_step, 0, 4), (4, q_step, 1, 3), (4, q_step, 2, 0), (6, q_step, 2, 1),
+        (7, q_step, 1, 4), (8, reduce_start, 0, 3), (8, q_step, 2, 2), (10, q_step, 2, 3),
+        (12, reduce_start, 1, 3), (12, reduce_next, 0), (12, q_step, 3, 0), (14, q_step, 3, 1),
+        (15, q_step, 2, 4), (15, reduce_direct, 0), (16, reduce_next, 1), (16, q_step, 3, 2),
+        (18, reduce_end, 0), (18, q_step, 3, 3), (19, reduce_direct, 1), (20, reduce_start, 2, 3),
+        (20, a_second, 0), (22, reduce_end, 1), (23, q_step, 3, 4), (23, a_step, 0, 3),
+        (24, reduce_next, 2), (24, a_second, 1), (26, reduce_direct, 2), (27, a_step, 1, 3),
+        (27, a_step, 0, 4), (28, reduce_start, 3, 3), (28, reduce_end, 2), (30, a_second, 2),
+        (31, a_step, 1, 4),
+    )
 
     load_v = pltpu.make_async_copy(cv_ref, vbuf, load_sem.at[0])
     load_k = pltpu.make_async_copy(ck_ref, kbuf, load_sem.at[1])
@@ -335,7 +364,7 @@
             at = (g * group_size + h) * HD
             qbuf[g, slot, h * rows : (h + 1) * rows] = turned(q_ref[:, at : at + HD])
     barrier_wait()
-    for g in range(groups):
+    for g in range(2):
         q_step(g, 0)
     for g in range(groups):
         knew[:, g * HD : (g + 1) * HD] = turned(kn_ref[:, g * HD : (g + 1) * HD])
@@ -409,21 +438,8 @@
 
     def step(t, unused):
         g, j = t // blocks, t % blocks
-        for i, stage in ((0, 2), (1, 3), (3, 4)):
-            pl.when(t == i)(functools.partial(q_step, 0, stage))
-        for i, stage in ((0, 1), (1, 2), (3, 3), (7, 4)):
-            pl.when((j == i) & (g < groups - 1))(functools.partial(q_step, g + 1, stage))
-        pl.when((j == 4) & (g > 0))(functools.partial(reduce_start, g, bits - 1))
-        pl.when(t == blocks)(functools.partial(reduce_start, 0, bits - 1))
-        for i, stage in ((3, 3), (5, 2), (6, 1), (7, 0)):
-            pl.when((j == i) & (g == 1))(functools.partial(reduce_step, 0, stage))
-        for i, stage in ((0, 3), (2, 2), (3, 1), (4, 0)):
-            pl.when((j == i) & (g > 1))(functools.partial(reduce_step, g - 1, stage))
-        for i, stage in ((0, 1), (1, 2), (2, 3), (5, 4)):
-            pl.when((j == i) & (g == 2))(functools.partial(a_step, 0, stage))
-        for i, stage in ((5, 1), (6, 2), (7, 3)):
-            pl.when((j == i) & (g > 1))(functools.partial(a_step, g - 1, stage))
-        pl.when((j == 2) & (g > 2))(functools.partial(a_step, g - 2, 4))
+        for at, act, *what in events:
+            pl.when(t == at)(functools.partial(act, *what))
         rb = block_at(g, j)
 
         now, later = t % 2, (t + 1) % 2
@@ -466,27 +482,20 @@
         proj[g % 2] = part if g < 2 else proj[g % 2] + part
 
     last = groups - 1
-    reduce_step(last, 3)
+    reduce_next(last)
     load_w.wait()
-    for g in range(last - 1):
-        project(g)
-    reduce_merge(last, 2)
-    for copy in last_copies(last):
-        copy.start()
-    a_step(last - 1, 4)
-    project(last - 1)
-    for copy in last_copies(last):
-        copy.wait_recv()
-    last_merge(last)
-    finish(last)
-    for copy in spread_copies(last, 0):
-        copy.start()
+    project(0)
+    a_step(last - 1, 3)
+    reduce_direct(last)
+    project(1)
+    reduce_end(last)
     for g in range(groups):
         att_ref[:, g * group_size * HD : (g + 1) * group_size * HD] = abuf[g, my_slot(g % 2)]
     for copy in spread_copies(last, 0):
         copy.wait_recv()
-    for copy in spread_copies(last, 1):
-        copy.start()
+    start_all(spread_copies(last, 1))
+    a_step(last - 1, 4)
+    project(last - 1)
     for copy in spread_copies(last, 1):
         copy.wait_recv()
     project(last)
@@ -516,16 +525,16 @@
         return 0
 
     def drain_rest(g, unused):
-        for stage in range(bits):
+        for stage in (2, 3):
             gather_copy(abuf, a_s, a_r, g, stage).wait_send()
-        for stage in (0, 1):
-            for copy in reduce_copies(g, stage):
-                copy.wait_send()
         return 0
 
     lax.fori_loop(0, groups, drain, 0)
     lax.fori_loop(0, last, drain_rest, 0)
-    for copy in last_copies(last) + spread_copies(last, 0) + spread_copies(last, 1):
+    for g in range(groups):
+        for copy in last_copies(g) + spread_copies(g, 0):
+            copy.wait_send()
+    for copy in spread_copies(last, 1):
         copy.wait_send()
 
 
@@ -590,8 +599,8 @@
             sems, sems, sems, sems, sems, sems, sems, sems,
             pltpu.SemaphoreType.DMA,
             pltpu.SemaphoreType.DMA,
-            pltpu.SemaphoreType.DMA((4, 3)),
-            pltpu.SemaphoreType.DMA((4, 3)),
+            pltpu.SemaphoreType.DMA((groups, 4, 3)),
+            pltpu.SemaphoreType.DMA((groups, 4, 3)),
         ],
         compiler_params=pltpu.CompilerParams(
             collective_id=0, has_side_effects=True, vmem_limit_bytes=60 * 2**20

time: 149 us -> 120 us (0.81)
  Pallas kernels: 141 us -> 112 us
    pallas_call x1, Pallas kernels: 141 us -> 112 us  [fused_device(): pl.pallas_call(functools.partial(fused_kernel, bits, groups, group_size,...]
where the time goes in v3:
time: 120 us
  Pallas kernels  112 us (93%)
  local copies, waits for them, and re-layouts  4.8 us (4%)
  other arithmetic  2.14 us (2%)
    pallas_call x1, Pallas kernels, fused_device(): pl.pallas_call(functools.partial(fused_kernel, bits, groups, group_size,...  112 us
    unnamed x2, local copies, waits for them, and re-layouts  3.14 us

profile of v3, /device:TPU:0, one launch (start us, length us, event | category | flops | bytes accessed | tf_op | source)
XLA Modules:
  0.0 119.5 jit_solution(12525260633842027839)
XLA Ops:
  0.6 0.8 fusion.1
  1.4 0.8 reshape.139
  2.2 0.1 stack_reshape.7
  2.3 0.1 stack_reshape.6
  2.4 0.6 pad_add_fusion.rinfo_ref
  3.0 0.1 multiply_cosine_fusion
  3.2 0.6 pad_maximum_fusion.trig_ref
  3.8 0.7 broadcast_in_dim.33.kpos_ref
  4.5 111.9 %shard_map.95 = (bf16[32,2048]{1,0:T(8,128)(2,1)}, bf16[256,256]{1,0:T(8,128)(2,1)}) custom-call(bf16[32,2048]{1,0:T(8,128)(2,1)} %q_ref.1, bf16[32,512]{1,0:T(8,128)(2,1)} %kn_ref.1, bf16[32,512]{1,0:T(8,128)(2,1)} %vn_ref.1, f32[2,32,128]{2,1,0:T(8,128)} %pad_maximum_fusion.trig_ref, s32[32,256]{1,0:T(8,128)} %broadcast_in_dim.33.kpos_ref, ...), custom_call_target="tpu_custom_call" | custom-call | tf_op jit(solution)/shard_map/pallas_call | solution.py:570
  116.4 1.6 %copy.15 = bf16[32,2048]{1,0:T(8,128)(2,1)} copy(bf16[32,2048]{1,0:T(8,128)(2,1)} %get-tuple-element.10) | data formatting | bytes 262144
  118.0 1.6 %copy.16 = bf16[256,256]{1,0:T(8,128)(2,1)} copy(bf16[256,256]{1,0:T(8,128)(2,1)} %get-tuple-element.11) | data formatting | bytes 262144
  (5 shorter events, 0.0 us)
